TPU v7x, 1024 devices: a whole 8x8x8 slice. The times are simulated.
1024 devices in a mesh: gx: 16 (over x, core), gy: 64 (over y, z).
Axes of the slice: x: 8, y: 8, z: 8, core: 2. Of those that a mesh axis runs over, the one named last changes fastest.
Arguments:
- displacement: float32 [3, 8, 512, 2048], P(None, None, 'gy', 'gx'), may hold values from -6 to 6
- velocity: float32 [3, 8, 512, 2048], P(None, None, 'gy', 'gx'), may hold values from -12 to 12
- body_force: float32 [3, 8, 512, 2048], P(None, None, 'gy', 'gx'), may hold values from -12 to 12
- modulus: float32 [8, 512, 2048], P(None, 'gy', 'gx'), may hold values from 0.5 to 2
- damage_bits: int32 [2, 8, 512, 2048], P(None, None, 'gy', 'gx'), may hold values from 0 to 255, as said below
Outputs:
- final_displacement: float32 [3, 8, 512, 2048], P(None, None, 'gy', 'gx')
- final_velocity: float32 [3, 8, 512, 2048], P(None, None, 'gy', 'gx')
Inputs may be any that keep to these rules, and one draw needn't show every extreme that they name: `damage_bits`: only bits 0 to 7 may be set.
All inputs are finite; a program needn't handle non-finite values.
Results may differ from a plain program's by a relative error of at most 0.015.
Values sent between devices are 32-bit elements; how exact they have to be, the bound alone decides.
A program may use at most 32 MiB of HBM per device.

v0:
```python
import math

import jax
import jax.numpy as jnp
from jax import lax
from jax.sharding import PartitionSpec as P

ITERS = 4


def padded(cells, sides, width):
    for axis, dim in sides:
        count = lax.axis_size(axis)
        ends = count - 1
        head = lax.slice_in_dim(cells, 0, width, axis=dim)
        tail = lax.slice_in_dim(cells, cells.shape[dim] - width, cells.shape[dim], axis=dim)
        cells = jnp.concatenate(
            [
                lax.ppermute(tail, axis, [(i, (i + 1) % count) for i in range(ends)]),
                cells,
                lax.ppermute(head, axis, [((i + 1) % count, i) for i in range(ends)]),
            ],
            axis=dim,
        )
    return cells


def from_behind(block, axis, distance):
    devices = range(lax.axis_size(axis))
    route = [(i - distance, i) for i in devices if i - distance in devices]
    return lax.ppermute(block, axis, route)


def half_offsets():
    result = []
    for step_x in range(-2, 3):
        for step_y in range(-2, 3):
            for step_z in range(-2, 3):
                length_sq = step_x * step_x + step_y * step_y + step_z * step_z
                leading = step_x if step_x != 0 else step_y if step_y != 0 else step_z
                if 0 < length_sq <= 4 and leading > 0:
                    result.append((step_x, step_y, step_z))
    return result


def mass_scale():
    return 2.0 * sum(
        (
            1.0 / math.sqrt(entry[0] * entry[0] + entry[1] * entry[1] + entry[2] * entry[2])
            for entry in half_offsets()
        )
    )


def shards(displacement, velocity, body_force, modulus, damage_bits):
    layer_count, row_count, column_count = modulus.shape
    offsets = half_offsets()
    fictive_mass = mass_scale()
    column_ids = lax.axis_index("gx") * column_count - 2 + jnp.arange(column_count + 4)
    column_inside = (column_ids >= 0) & (column_ids < column_count * lax.axis_size("gx"))
    row_ids = lax.axis_index("gy") * row_count - 2 + jnp.arange(row_count + 4)
    row_inside = (row_ids >= 0) & (row_ids < row_count * lax.axis_size("gy"))
    layer_ids = jnp.arange(layer_count + 4) - 2
    layer_inside = (layer_ids >= 0) & (layer_ids < layer_count)
    inside_mask = (
        layer_inside[:, None, None] & row_inside[None, :, None] & column_inside[None, None, :]
    ).astype(jnp.float32)

    def extend(vector_field):
        rows_ext = padded(vector_field, (("gy", 2),), 2)
        ahead = from_behind(rows_ext[:, :, :, :2], "gx", -1)
        blank = jnp.zeros(rows_ext.shape[:3] + (2,), rows_ext.dtype)
        rimmed = jnp.concatenate([blank, rows_ext, ahead], axis=3)
        return jnp.pad(rimmed, ((0, 0), (2, 2), (0, 0), (0, 0)))

    initial = extend(jnp.concatenate([displacement, modulus[None]], axis=0))
    modulus_ext = initial[3]
    interior = (slice(2, 2 + layer_count), slice(2, 2 + row_count), slice(2, 2 + column_count))
    modulus_own = modulus_ext[interior]

    def shifted(step, sign):
        return (
            slice(2 + sign * step[2], 2 + sign * step[2] + layer_count),
            slice(2 + sign * step[1], 2 + sign * step[1] + row_count),
            slice(2 + sign * step[0], 2 + sign * step[0] + column_count),
        )

    def bond_term(field_ext, own_values, window, bits_here, number, step):
        partner = field_ext[(slice(None),) + window]
        stretch = (
            step[0] * (partner[0] - own_values[0])
            + step[1] * (partner[1] - own_values[1])
            + step[2] * (partner[2] - own_values[2])
        )
        broken = jnp.bitwise_and(jnp.right_shift(bits_here[number // 8], number % 8), 1).astype(
            jnp.float32
        )
        length = math.sqrt(step[0] * step[0] + step[1] * step[1] + step[2] * step[2])
        stiffness = (
            0.5
            * (modulus_own + modulus_ext[window])
            * (1.0 - broken)
            * inside_mask[window]
            / (length * length * length)
        )
        return (stiffness * stretch, stretch)

    def carry_rows(ghost_rows, distance):
        return from_behind(ghost_rows, "gy", distance)

    def bond_forces(field_ext):
        own_values = field_ext[(slice(None),) + interior]
        own_sum = jnp.zeros_like(own_values)
        spread_forces = jnp.zeros_like(field_ext)
        energy = jnp.zeros((), jnp.float32)
        for number, step in enumerate(offsets):
            window = shifted(step, 1)
            magnitude, stretch = bond_term(field_ext, own_values, window, damage_bits, number, step)
            bond_pull = jnp.stack([magnitude * step[0], magnitude * step[1], magnitude * step[2]])
            own_sum = own_sum + bond_pull
            spread_forces = spread_forces.at[(slice(None),) + window].add(-bond_pull)
        spread_forces = spread_forces.at[(slice(None),) + interior].add(own_sum)
        ghost_strip = spread_forces[:, 2 : 2 + layer_count, :, column_count + 2 :]
        arrived = from_behind(ghost_strip, "gx", 1)
        spread_forces = spread_forces.at[:, 2 : 2 + layer_count, :, 2:4].add(arrived)
        core_block = spread_forces[:, 2 : 2 + layer_count, :, 2 : 2 + column_count]
        upper = carry_rows(core_block[:, :, row_count + 2 :, :], 1)
        lower = carry_rows(core_block[:, :, :2, :], -1)
        result = core_block[:, :, 2 : 2 + row_count, :]
        result = result.at[:, :, :2, :].add(upper)
        result = result.at[:, :, row_count - 2 :, :].add(lower)
        return (result, energy)

    forces, unused = bond_forces(initial[:3])
    current = displacement
    velocity_now = velocity
    for iteration in range(ITERS):
        change, unused = bond_forces(extend(velocity_now))
        numerator_part = -jnp.sum(velocity_now * change) / fictive_mass
        if iteration > 0:
            forces = forces + change
        numerator, denominator = lax.psum(
            (numerator_part, jnp.sum(velocity_now * velocity_now)), ("gx", "gy")
        )
        damping = 2.0 * jnp.sqrt(numerator / (denominator + 1e-06))
        velocity_now = (
            (2.0 - damping) * velocity_now + 2.0 * (forces + body_force) / fictive_mass
        ) / (2.0 + damping)
        current = current + velocity_now
    return (current, velocity_now)


def solution(mesh):
    placed = (
        P(None, None, "gy", "gx"),
        P(None, None, "gy", "gx"),
        P(None, None, "gy", "gx"),
        P(None, "gy", "gx"),
        P(None, None, "gy", "gx"),
    )
    return jax.shard_map(
        shards,
        mesh=mesh,
        in_specs=placed,
        out_specs=(P(None, None, "gy", "gx"), P(None, None, "gy", "gx")),
        check_vma=False,
    )
```

profile of v0, /device:TPU:1, one launch (start us, length us, event | category | flops | bytes accessed | tf_op | source)
XLA Modules:
  0.0 1293.0 jit_solution(17239307600964255949)
XLA Ops:
  17.5 10.6 collective-permute-start.5
  48.4 8.0 scatter-add.369
  56.5 7.5 scatter-add.370
  73.8 7.5 scatter-add.374
  81.5 7.5 scatter-add.375
  89.1 7.5 scatter-add.376
  96.8 7.5 scatter-add.379
  104.4 7.5 scatter-add.380
  119.8 7.5 scatter-add.384
  142.9 7.5 scatter-add.389
  166.0 7.5 scatter-add.394
  176.3 7.7 scatter-add.335
  184.2 7.5 scatter-add.336
  191.8 7.5 scatter-add.339
  207.1 7.5 scatter-add.341
  214.7 7.5 scatter-add.344
  230.0 7.5 scatter-add.346
  260.5 7.5 scatter-add.354
  268.2 7.5 scatter-add.355
  291.1 7.5 scatter-add.360
  325.4 130.3 %all-reduce.13 = (f32[]{:T(128)}, f32[]{:T(128)}) all-reduce(f32[]{:T(128)S(6)} %div.81, f32[]{:T(128)} %get-tuple-element.1208), channel_id=1, replica_groups=mesh['gx'=16,'gy'=64] {'gx','gy'}, use_global_device_ids=true, to_apply=%region_1.2 | all-reduce | flops 2 | bytes 16 | tf_op jit(solution)/shard_map/psum | solution.py:142
  612.5 120.9 %all-reduce.12 = (f32[]{:T(128)}, f32[]{:T(128)}) all-reduce(f32[]{:T(128)S(6)} %div.87, f32[]{:T(128)} %get-tuple-element.1206), channel_id=1, replica_groups=mesh['gx'=16,'gy'=64] {'gx','gy'}, use_global_device_ids=true, to_apply=%region_5.6 | all-reduce | flops 2 | bytes 16 | tf_op jit(solution)/shard_map/psum | solution.py:142
  890.0 122.3 %all-reduce.11 = (f32[]{:T(128)}, f32[]{:T(128)}) all-reduce(f32[]{:T(128)S(6)} %div.92, f32[]{:T(128)} %get-tuple-element.1204), channel_id=1, replica_groups=mesh['gx'=16,'gy'=64] {'gx','gy'}, use_global_device_ids=true, to_apply=%region_9.10 | all-reduce | flops 2 | bytes 16 | tf_op jit(solution)/shard_map/psum | solution.py:142
  1168.6 122.2 %all-reduce.10 = (f32[]{:T(128)}, f32[]{:T(128)}) all-reduce(f32[]{:T(128)S(6)} %div.97, f32[]{:T(128)} %get-tuple-element.1202), channel_id=1, replica_groups=mesh['gx'=16,'gy'=64] {'gx','gy'}, use_global_device_ids=true, to_apply=%region_13.14 | all-reduce | flops 2 | bytes 16 | tf_op jit(solution)/shard_map/psum | solution.py:142
  (425 shorter events, 631.6 us)
Async XLA Ops:
  1.6 15.8 %collective-permute-start.3 = (f32[3,8,2,128]{3,2,1,0:T(2,128)S(1)}, f32[3,8,2,128]{3,2,1,0:T(2,128)S(1)}, u32[]{:S(2)}, u32[]{:S(2)}) collective-permute-start(f32[3,8,2,128]{3,2,1,0:T(2,128)S(1)} %get-tuple-element.1507), channel_id=1, source_target_pairs={{0,1},{1,2},{2,3},{3,4},{4,5},{5,6},{6,7},{7,8},{8,9},{9,10},{10,1... | collective-permute-start | bytes 73736 | tf_op jit(solution)/shard_map/ppermute | solution.py:19
  7.4 10.1 collective-permute-start.4
  9.5 20.0 %collective-permute-start = (f32[4,8,2,128]{3,2,1,0:T(2,128)S(1)}, f32[4,8,2,128]{3,2,1,0:T(2,128)S(1)}, u32[]{:S(2)}, u32[]{:S(2)}) collective-permute-start(f32[4,8,2,128]{3,2,1,0:T(2,128)S(1)} %get-tuple-element.1485), channel_id=1, source_target_pairs={{0,1},{1,2},{2,3},{3,4},{4,5},{5,6},{6,7},{7,8},{8,9},{9,10},{10,1... | collective-permute-start | bytes 98312 | tf_op jit(solution)/shard_map/ppermute | solution.py:19
  15.1 14.4 %collective-permute-start.1 = (f32[4,8,2,128]{3,2,1,0:T(2,128)S(1)}, f32[4,8,2,128]{3,2,1,0:T(2,128)S(1)}, u32[]{:S(2)}, u32[]{:S(2)}) collective-permute-start(f32[4,8,2,128]{3,2,1,0:T(2,128)S(1)} %get-tuple-element.1486), channel_id=1, source_target_pairs={{1,0},{2,1},{3,2},{4,3},{5,4},{6,5},{7,6},{8,7},{9,8},{10,9},{11,1... | collective-permute-start | bytes 98312 | tf_op jit(solution)/shard_map/ppermute | solution.py:21
  17.5 11.7 collective-permute-start.5
  29.6 7.7 collective-permute-start.2
  173.6 127.1 %collective-permute-start.9 = (f32[3,8,12,2]{3,2,1,0:T(8,128)S(1)}, f32[3,8,12,2]{3,2,1,0:T(8,128)}, u32[]{:S(2)}, u32[]{:S(2)}) collective-permute-start(f32[3,8,12,2]{3,2,1,0:T(8,128)S(1)} %slice.5966), channel_id=1, source_target_pairs={{0,64},{64,128},{128,192},{192,256},{256,320},{320,384},{384,448},... | collective-permute-start | bytes 6920 | tf_op jit(solution)/shard_map/ppermute | solution.py:31
  298.8 11.2 collective-permute-start.6
  305.7 17.7 %collective-permute-start.10 = (f32[3,8,2,128]{3,2,1,0:T(2,128)S(1)}, f32[3,8,2,128]{3,2,1,0:T(2,128)S(1)}, u32[]{:S(2)}, u32[]{:S(2)}) collective-permute-start(f32[3,8,2,128]{3,2,1,0:T(2,128)S(1)} %get-tuple-element.1436), channel_id=1, source_target_pairs={{0,1},{1,2},{2,3},{3,4},{4,5},{5,6},{6,7},{7,8},{8,9},{9,10},{10,1... | collective-permute-start | bytes 73736 | tf_op jit(solution)/shard_map/ppermute | solution.py:31
  314.2 142.9 %collective-permute-start.11 = (f32[3,8,2,128]{3,2,1,0:T(2,128)S(1)}, f32[3,8,2,128]{3,2,1,0:T(2,128)S(1)}, u32[]{:S(2)}, u32[]{:S(2)}) collective-permute-start(f32[3,8,2,128]{3,2,1,0:T(2,128)S(1)} %get-tuple-element.1435), channel_id=1, source_target_pairs={{1,0},{2,1},{3,2},{4,3},{5,4},{6,5},{7,6},{8,7},{9,8},{10,9},{11,1... | collective-permute-start | bytes 73736 | tf_op jit(solution)/shard_map/ppermute | solution.py:31
  315.5 8.5 collective-permute-start.8
  316.8 7.1 collective-permute-start.7
  459.7 4.6 collective-permute-start.13
  464.3 7.5 collective-permute-start.14
  595.3 4.5 collective-permute-start.15
  606.6 4.6 collective-permute-start.17
  736.0 4.6 collective-permute-start.19
  740.7 9.7 collective-permute-start.20
  873.8 4.5 collective-permute-start.21
  884.1 4.6 collective-permute-start.23
  1015.0 4.6 collective-permute-start.25
  1019.6 9.3 collective-permute-start.26
  1152.4 4.5 collective-permute-start.27
  1162.7 4.6 collective-permute-start.29
  (44 other events, 370.8 us)
where the time goes:
time: 1300 us; the launch traced here: 1290 us
  local copies, waits for them, and re-layouts  628 us (48%)
  blocking collectives  496 us (38%)
  starting transfers between devices  81.2 us (6%)
  waiting for transfers between devices  47.5 us (4%)
  other arithmetic  29.1 us (2%)
    scatter-add x80, local copies, waits for them, and re-layouts, bond_forces(): spread_forces = spread_forces.at[(slice(None),) + window].add(-bond_pull)  565 us
    psum x4, blocking collectives, shards(): lax.psum((numerator_part, jnp.sum(velocity_now * velocity_now)), ('gx', '...  496 us
    ppermute x20, starting transfers between devices, from_behind(): return lax.ppermute(block, axis, route)  58.4 us
    ppermute x20, waiting for transfers between devices, from_behind(): return lax.ppermute(block, axis, route)  37.7 us
    scatter-add x5, local copies, waits for them, and re-layouts, bond_forces(): spread_forces = spread_forces.at[(slice(None),) + interior].add(own_sum)  37.6 us
  transfers between devices with their start and end apart: 30, of which 15 were waited for; matrix products, arithmetic and copies ran while one was open for 10% of the time, Pallas kernels for 0%

commit v1 on v0

v1 whole, which is shorter than its diff:
```python
import functools
import math

import jax
import jax.numpy as jnp
from jax import lax
from jax.experimental import pallas as pl
from jax.experimental.pallas import tpu as pltpu
from jax.sharding import PartitionSpec as P

ITERS = 4
STEPS = ITERS
NZ, NY, NX = 8, 8, 128
GX, GY, GZ = 16, 8, 8
MESH = pl.DeviceIdType.MESH
F32 = jnp.float32


def half_offsets():
    result = []
    for step_x in range(-2, 3):
        for step_y in range(-2, 3):
            for step_z in range(-2, 3):
                length_sq = step_x * step_x + step_y * step_y + step_z * step_z
                leading = step_x if step_x != 0 else step_y if step_y != 0 else step_z
                if 0 < length_sq <= 4 and leading > 0:
                    result.append((step_x, step_y, step_z))
    return result


HALF = half_offsets()
FULL = [(entry, number, 1) for number, entry in enumerate(HALF)] + [
    (tuple(-part for part in entry), number, -1) for number, entry in enumerate(HALF)
]
BOND = {entry: place for place, (entry, _, _) in enumerate(FULL)}
FICTIVE_MASS = 2.0 * sum(1.0 / math.sqrt(a * a + b * b + c * c) for a, b, c in HALF)

SIDES = [(-1, 0), (1, 0), (-1, -1), (1, -1), (-1, 1), (1, 1)]


def hops(distance, count):
    return min(distance % count, -distance % count)


X_PARTNERS = sorted(range(1, GX), key=lambda d: -hops(d, GX))
YZ_PARTNERS = sorted(
    [(dy, dz) for dy in range(GY) for dz in range(GZ) if dy or dz],
    key=lambda d: -(hops(d[0], GY) + hops(d[1], GZ)),
)

VV = [18, 0, 1, 6, 7, 12]
GG = [3, 8, 9, 14, 15, 19]
VG = [4, 5, 10, 11, 16, 17]
SLOTS = 24


def kernel(
    u_hbm, v_hbm, body_hbm, mod_hbm, bits_hbm, u_out, v_out,
    raw_u, raw_v, raw_body, raw_mod, raw_bits,
    field, static, ahead, behind, ahead2, behind2, stiff, sides_static, last,
    edge_out, edge_in, inner_in, static_in, moments, row_out, row_x, row_yz,
    load_sem, y_send, y_recv, e_send, e_recv, i_send, i_recv, s_send, s_recv, sy_send, sy_recv,
    rx_send, rx_recv, ryz_send, ryz_recv,
):
    gx, gy = lax.axis_index("gx"), lax.axis_index("gy")
    part_y, part_z = gy // GZ, gy % GZ

    def near(dx, dy):
        return ((gx + dx + GX) % GX, (gy + dy + GY * GZ) % (GY * GZ))

    x_partners = [((gx + d) % GX, gy) for d in X_PARTNERS]
    yz_partners = [
        (gx, ((part_y + dy) % GY) * GZ + (part_z + dz) % GZ) for dy, dz in YZ_PARTNERS
    ]
    near_all = [(dx, dy) for dx in (-1, 0, 1) for dy in (-1, 0, 1) if dx or dy]
    barrier = pltpu.get_barrier_semaphore()
    greeted = [near(dx, dy) for dx, dy in near_all] + x_partners + yz_partners
    for device in greeted:
        pl.semaphore_signal(barrier, inc=1, device_id=device, device_id_type=MESH)

    loads = [
        pltpu.make_async_copy(source, target, load_sem.at[place])
        for place, (source, target) in enumerate(
            [(u_hbm, raw_u), (v_hbm, raw_v), (mod_hbm, raw_mod), (bits_hbm, raw_bits), (body_hbm, raw_body)]
        )
    ]
    for load in loads:
        load.start()

    lane = lax.broadcasted_iota(jnp.int32, (NZ, NX), 1)
    layer = lax.broadcasted_iota(jnp.int32, (NZ, NX), 0)

    def lanes_on(value, amount):
        return pltpu.roll(value, (-amount) % NX, axis=1)

    def layers_on(value, amount):
        return value if amount == 0 else pltpu.roll(value, (-amount) % NZ, axis=0)

    def pack(values):
        total = jnp.zeros((NZ, NX), F32)
        for place, value in enumerate(values):
            total = jnp.where(lane // 4 == place, pltpu.roll(value, (4 * place + 2) % NX, axis=1), total)
        return total

    def joined(left, right):
        return jnp.where(lane % 4 < 2, left, right)

    def rim(both, place):
        return pltpu.roll(both, (2 * NX - 4 * place - 2) % NX, axis=1)

    def plus(value, halo, amount):
        if amount > 0:
            return lanes_on(jnp.where(lane < amount, halo, value), amount)
        return lanes_on(jnp.where(lane >= NX + amount, halo, value), amount)

    def remote(source, target, send, recv, device):
        return pltpu.make_async_remote_copy(
            src_ref=source, dst_ref=target, send_sem=send, recv_sem=recv,
            device_id=device, device_id_type=MESH,
        )

    def y_copies(step):
        return [
            remote(field.at[step, :, :, 9], field.at[step, :, :, 1], y_send.at[step, 0], y_recv.at[step, 0], near(0, 1)),
            remote(field.at[step, :, :, 2], field.at[step, :, :, 10], y_send.at[step, 1], y_recv.at[step, 1], near(0, -1)),
            remote(field.at[step, :, 1, 8], field.at[step, :, 1, 0], y_send.at[step, 2], y_recv.at[step, 2], near(0, 1)),
            remote(field.at[step, :, 1, 3], field.at[step, :, 1, 11], y_send.at[step, 3], y_recv.at[step, 3], near(0, -1)),
        ]

    def static_y_copies():
        return [
            remote(static.at[:, 9], static.at[:, 1], sy_send.at[0], sy_recv.at[0], near(0, 1)),
            remote(static.at[:, 2], static.at[:, 10], sy_send.at[1], sy_recv.at[1], near(0, -1)),
            remote(static.at[0:2, 8], static.at[0:2, 0], sy_send.at[2], sy_recv.at[2], near(0, 1)),
            remote(static.at[0:1, 3], static.at[0:1, 11], sy_send.at[3], sy_recv.at[3], near(0, -1)),
        ]

    def edge_copies(step, source, target, send, recv, count):
        return [
            remote(source, target.at[step, place], send.at[step, place], recv.at[step, place], near(-dx, -dy))
            for place, (dx, dy) in reversed(list(enumerate(SIDES[:count])))
        ]

    def boundary_copies(step):
        return edge_copies(step, edge_out.at[step, 0], edge_in, e_send, e_recv, 6)

    def inner_copies(step):
        return edge_copies(step, edge_out.at[step, 1], inner_in, i_send, i_recv, 2)

    def static_copies():
        return edge_copies(0, sides_static, static_in, s_send, s_recv, 6)

    BOUNDARY = (0, 1, 6, 7)
    INNER = (2, 3, 4, 5)

    def pack_rows(step, rows):
        return pack([field[step, f, c, 2 + y] for y in rows for f in range(2) for c in range(3)])

    for load in loads[:4]:
        load.wait()
    for y in range(NY):
        turned = pl.ds(y, NZ, stride=NY)
        for c in range(3):
            field[0, 0, c, 2 + y] = raw_u[c, turned, :]
            field[0, 1, c, 2 + y] = raw_v[c, turned, :]
        static[0, 2 + y] = raw_mod[turned, :]
        for c in range(2):
            static[1 + c, 2 + y] = raw_bits[c, turned, :].astype(F32)
    edge_out[0, 0] = pack_rows(0, BOUNDARY)
    edge_out[0, 1] = pack_rows(0, INNER)
    sides_static[...] = pack([static[c, 2 + y] for y in range(NY) for c in range(3)])

    pl.semaphore_wait(barrier, len(greeted))
    for copy in static_y_copies() + static_copies() + y_copies(0) + boundary_copies(0) + inner_copies(0):
        copy.start()
    loads[4].wait()

    for copy in static_y_copies() + static_copies():
        copy.wait_recv()
    edge = {-1: joined(static_in[0, 2], static_in[0, 3]), 0: joined(static_in[0, 0], static_in[0, 1]), 1: joined(static_in[0, 4], static_in[0, 5])}
    for y in range(-1, NY + 1):
        side = -1 if y < 0 else 1 if y >= NY else 0
        row = y - side * NY
        for c in range(3):
            value, halo = static[c, 2 + y], rim(edge[side], 3 * row + c)
            if c == 0:
                ahead[1, 0, 0, 1 + y] = plus(value, halo, 1)
            behind[1, 0, c, 1 + y] = plus(value, halo, -1)
            if side == 0 and c == 0:
                ahead2[1, 0, y] = plus(value, halo, 2)
            if side == 0 and c != 1:
                behind2[1, c // 2, y] = plus(value, halo, -2)

    column_on = {}
    for a in range(-2, 3):
        on = jnp.logical_and(
            jnp.logical_or(gx > 0, lane + a >= 0), jnp.logical_or(gx < GX - 1, lane + a < NX)
        )
        column_on[a] = on
    layer_on = {c: jnp.logical_and(layer + c >= 0, layer + c < NZ) for c in range(-2, 3)}
    weight = {}
    for a, b, c in BOND:
        if (a, c) not in weight:
            weight[a, c] = jnp.logical_and(column_on[a], layer_on[c]).astype(F32)

    def stiff_row(y, carry):
        def mod_at(a, b):
            if a == 0:
                return static[0, 2 + y + b]
            if abs(a) == 1:
                return (ahead if a > 0 else behind)[1, 0, 0, 1 + y + b]
            return (ahead2 if a > 0 else behind2)[1, 0, y]

        def bits_at(word, a, b):
            if a == 0:
                value = static[1 + word, 2 + y + b]
            elif a == -1:
                value = behind[1, 0, 1 + word, 1 + y + b]
            else:
                value = behind2[1, 1, y]
            return value.astype(jnp.int32)

        row_on = {}
        for b in range(-2, 3):
            on = jnp.logical_and(
                jnp.logical_or(gy > 0, y + b >= 0), jnp.logical_or(gy < GY * GZ - 1, y + b < NY)
            )
            row_on[b] = jnp.where(on, 1.0, 0.0).astype(F32)
        own = static[0, 2 + y]
        words = {}
        partners = {}
        for place, ((a, b, c), number, sign) in enumerate(FULL):
            if (a, b, c) not in partners:
                partners[a, b, c] = layers_on(mod_at(a, b), c)
            length_sq = a * a + b * b + c * c
            scale = 0.5 / (length_sq * math.sqrt(length_sq))
            if length_sq == 4:
                scale = scale * 4.0
            value = (own + partners[a, b, c]) * (weight[a, c] * (row_on[b] * scale))
            where = (number // 8, a, b) if sign < 0 else (number // 8, 0, 0)
            if where not in words:
                words[where] = bits_at(*where)
            broken = jnp.bitwise_and(words[where], 1 << (number % 8))
            if sign < 0:
                broken = layers_on(broken, c)
            stiff[place, y] = jnp.where(broken == 0, value, 0.0)
        return carry

    lax.fori_loop(0, NY, stiff_row, 0)

    def widen(step, fields, y, edge_side, place):
        for f in fields:
            for c in range(3):
                value, halo = field[step, f, c, 2 + y], rim(edge_side, place + 3 * f + c)
                ahead[0, f, c, 1 + y] = plus(value, halo, 1)
                behind[0, f, c, 1 + y] = plus(value, halo, -1)
                if c == 0 and 0 <= y < NY:
                    ahead2[0, f, y] = plus(value, halo, 2)
                    behind2[0, f, y] = plus(value, halo, -2)

    def row_force(step, f, y):
        own = [field[step, f, c, 2 + y] for c in range(3)]
        force = [jnp.zeros((NZ, NX), F32) for _ in range(3)]

        def bond(a, b, c):
            return stiff[BOND[a, b, c], y]

        for c in (-1, 1, -2, 2):
            force[2] += bond(0, 0, c) * (layers_on(own[2], c) - own[2])
        for b in (-1, 1):
            pair = [None if c == 0 else field[step, f, c, 2 + y + b] for c in range(3)]
            pulls = {}
            for gamma in (-1, 0, 1):
                c = gamma * b
                partner = pair[1] + gamma * pair[2] if gamma else pair[1]
                mine = own[1] + gamma * own[2] if gamma else own[1]
                pulls[gamma] = bond(0, b, c) * (layers_on(partner, c) - mine)
            force[1] += pulls[-1] + pulls[0] + pulls[1]
            force[2] += pulls[1] - pulls[-1]
        for b in (-2, 2):
            force[1] += bond(0, b, 0) * (field[step, f, 1, 2 + y + b] - own[1])
        force[0] += bond(2, 0, 0) * (ahead2[0, f, y] - own[0])
        force[0] += bond(-2, 0, 0) * (behind2[0, f, y] - own[0])
        for beta in (-1, 0, 1):
            mine = own[0] + beta * own[1] if beta else own[0]
            for a in (-1, 1):
                b = a * beta
                source = ahead if a > 0 else behind
                pair = [source[0, f, c, 1 + y + b] for c in range(3)]
                partner = pair[0] + beta * pair[1] if beta else pair[0]
                pulls = {}
                for gamma in (-1, 0, 1):
                    c = gamma * a
                    there = partner + gamma * pair[2] if gamma else partner
                    here = mine + gamma * own[2] if gamma else mine
                    pulls[gamma] = bond(a, b, c) * (layers_on(there, c) - here)
                total = pulls[-1] + pulls[0] + pulls[1]
                force[0] += total
                if beta:
                    force[1] += beta * total
                force[2] += pulls[1] - pulls[-1]
        return own, force

    def dot(first, second):
        return first[0] * second[0] + first[1] * second[1] + first[2] * second[2]

    def rows_pass(step, first_row):
        body_on = jnp.where(step == 0, 1.0, 0.0).astype(F32)

        def row(index, sums):
            y = first_row(index)
            old_g, new_g = row_force(step, 0, y)
            for c in range(3):
                new_g[c] = new_g[c] + body_on * raw_body[c, pl.ds(y, NZ, stride=NY), :]
                field[step + 1, 0, c, 2 + y] = new_g[c]
            old_v, new_v = row_force(step, 1, y)
            for c in range(3):
                field[step + 1, 1, c, 2 + y] = new_v[c]
            terms = [
                dot(old_v, new_v), dot(new_v, new_v), dot(old_g, new_g),
                dot(new_g, new_g), dot(old_v, new_g), dot(new_v, new_g),
            ]
            return tuple(total + term for total, term in zip(sums, terms))

        sums = lax.fori_loop(0, 4, row, (jnp.zeros((NZ, NX), F32),) * 6)
        return sums

    def arrive(step, fields):
        for copy in edge_copies(step, edge_out.at[step, 0], edge_in, e_send, e_recv, 2) + inner_copies(step):
            copy.wait_recv()
        near_edge = joined(edge_in[step, 0], edge_in[step, 1])
        near_inner = joined(inner_in[step, 0], inner_in[step, 1])
        for place, y in enumerate(BOUNDARY):
            widen(step, fields, y, near_edge, 6 * place)
        for place, y in enumerate(INNER):
            widen(step, fields, y, near_inner, 6 * place)
        for copy in boundary_copies(step)[:4] + y_copies(step):
            copy.wait_recv()
        widen(step, fields, -1, joined(edge_in[step, 2], edge_in[step, 3]), 18)
        widen(step, fields, NY, joined(edge_in[step, 4], edge_in[step, 5]), 0)

    def outer_row(index):
        return index + 4 * (index // 2)

    def inner_row(index):
        return index + 2

    def advance(step, carry):
        arrive(step, (0, 1))
        outer = rows_pass(step, outer_row)
        for copy in y_copies(step + 1):
            copy.start()
        edge_out[step + 1, 0] = pack_rows(step + 1, BOUNDARY)
        for copy in boundary_copies(step + 1):
            copy.start()
        inner = rows_pass(step, inner_row)
        edge_out[step + 1, 1] = pack_rows(step + 1, INNER)
        for copy in inner_copies(step + 1):
            copy.start()
        for place in range(6):
            moments[step * 6 + place] = outer[place] + inner[place]
        return carry

    lax.fori_loop(0, STEPS - 1, advance, 0)

    final = STEPS - 1
    arrive(final, (0,))

    def last_row(y, total):
        old, new = row_force(final, 0, y)
        for c in range(3):
            last[c, y] = new[c]
        return total + dot(old, new)

    moments[19] = lax.fori_loop(0, NY, last_row, jnp.zeros((NZ, NX), F32))
    start_v = [[field[0, 1, c, 2 + y] for c in range(3)] for y in range(NY)]
    moments[18] = sum(dot(value, value) for value in start_v)
    for place in range(20, SLOTS):
        moments[place] = jnp.zeros((NZ, NX), F32)

    wide_lane = lax.broadcasted_iota(jnp.int32, (SLOTS, NX), 1)
    wide_row = lax.broadcasted_iota(jnp.int32, (SLOTS, NX), 0)
    summed = jnp.sum(jnp.sum(moments[...], axis=1), axis=1, keepdims=True)
    flat = jnp.sum(jnp.where(wide_lane == wide_row, summed, 0.0), axis=0, keepdims=True)

    def exchange(value, rows, partners, out, send, recv):
        count = len(partners)
        row_out[out, 0:1] = value
        rows[count : count + 1] = value
        for place, device in enumerate(partners):
            remote(row_out.at[out, 0:1], rows.at[place : place + 1], send, recv, device).start()
        whole = rows.at[0:count]
        pltpu.make_async_copy(whole, whole, recv).wait()
        total = jnp.sum(rows[...], axis=0, keepdims=True)
        pltpu.make_async_copy(whole, whole, send).wait()
        return total

    flat = exchange(flat, row_x, x_partners, 0, rx_send, rx_recv)
    flat = exchange(flat, row_yz, yz_partners, 1, ryz_send, ryz_recv)

    spread = jnp.sum(jnp.where(wide_lane == wide_row, jnp.broadcast_to(flat, (SLOTS, NX)), 0.0), axis=1, keepdims=True)
    spread = jnp.broadcast_to(spread, (SLOTS, NX))
    vv, gg, vg = ([spread[place : place + 1] for place in places] for places in (VV, GG, VG))

    zero = jnp.zeros((1, NX), F32)
    one = jnp.ones((1, NX), F32)
    speed_v, speed_g = [one, zero, zero, zero], [zero] * 4
    pull_v, pull_g = [zero] * 4, [one, zero, zero, zero]
    path_v, path_g = [zero] * 4, [zero] * 4
    for n in range(ITERS):
        terms = range(n if n else 1)

        def quadratic(order):
            total = zero
            for i in terms:
                for j in terms:
                    total = total + speed_v[i] * speed_v[j] * vv[i + j + order]
                    if n:
                        total = total + 2.0 * speed_v[i] * speed_g[j] * vg[i + j + order]
                        total = total + speed_g[i] * speed_g[j] * gg[i + j + order]
            return total

        denominator = quadratic(0)
        numerator = jnp.maximum(-quadratic(1) / FICTIVE_MASS, 0.0)
        damping = 2.0 * jnp.sqrt(numerator / (denominator + 1e-06))
        keep = (2.0 - damping) / (2.0 + damping)
        gain = 2.0 / (FICTIVE_MASS * (2.0 + damping))
        speed_v = [keep * x + gain * y for x, y in zip(speed_v, pull_v)]
        speed_g = [keep * x + gain * y for x, y in zip(speed_g, pull_g)]
        path_v = [x + y for x, y in zip(path_v, speed_v)]
        path_g = [x + y for x, y in zip(path_g, speed_g)]
        pull_v = [pull_v[0]] + [pull_v[j] + speed_v[j - 1] for j in range(1, 4)]
        pull_g = [pull_g[0]] + [pull_g[j] + speed_g[j - 1] for j in range(1, 4)]

    weights = [[jnp.broadcast_to(x, (NZ, NX)) for x in group] for group in (speed_v, speed_g, path_v, path_g)]

    def finish_row(y, carry):
        turned = pl.ds(y, NZ, stride=NY)
        for c in range(3):
            velocities = [field[j, 1, c, 2 + y] for j in range(4)]
            forces = [field[j + 1, 0, c, 2 + y] for j in range(3)] + [last[c, y]]
            v_new = sum(w * x for w, x in zip(weights[0] + weights[1], velocities + forces))
            moved = sum(w * x for w, x in zip(weights[2] + weights[3], velocities + forces))
            v_out[c, turned, :] = v_new
            u_out[c, turned, :] = field[0, 0, c, 2 + y] + moved
        return carry

    lax.fori_loop(0, NY, finish_row, 0)

    for copy in static_y_copies() + static_copies():
        copy.wait_send()

    def drain(step, carry):
        for copy in y_copies(step) + boundary_copies(step) + inner_copies(step):
            copy.wait_send()
        return carry

    lax.fori_loop(0, STEPS, drain, 0)


def shards(displacement, velocity, body_force, modulus, damage_bits):
    rows = NZ * NY
    vmem = pltpu.VMEM
    dma = pltpu.SemaphoreType.DMA
    block = (NZ, NX)
    out = jax.ShapeDtypeStruct((3, rows, NX), F32)
    u, v = pl.pallas_call(
        kernel,
        name="relax",
        out_shape=(out, out),
        in_specs=[pl.BlockSpec(memory_space=pl.ANY)] * 5,
        out_specs=[pl.BlockSpec(memory_space=vmem)] * 2,
        scratch_shapes=[
            vmem((3, rows, NX), F32), vmem((3, rows, NX), F32), vmem((3, rows, NX), F32),
            vmem((rows, NX), F32), vmem((2, rows, NX), jnp.int32),
            vmem((STEPS, 2, 3, NY + 4) + block, F32),
            vmem((3, NY + 4) + block, F32),
            vmem((2, 2, 3, NY + 2) + block, F32),
            vmem((2, 2, 3, NY + 2) + block, F32),
            vmem((2, 2, NY) + block, F32),
            vmem((2, 2, NY) + block, F32),
            vmem((len(FULL), NY) + block, F32),
            vmem(block, F32),
            vmem((3, NY) + block, F32),
            vmem((STEPS, 2) + block, F32),
            vmem((STEPS, 6) + block, F32),
            vmem((STEPS, 2) + block, F32),
            vmem((1, 6) + block, F32),
            vmem((SLOTS,) + block, F32),
            vmem((2, 8, NX), F32),
            vmem((GX, NX), F32),
            vmem((GY * GZ, NX), F32),
            dma((5,)),
            dma((STEPS, 4)), dma((STEPS, 4)),
            dma((STEPS, 6)), dma((STEPS, 6)),
            dma((STEPS, 2)), dma((STEPS, 2)),
            dma((1, 6)), dma((1, 6)),
            dma((4,)), dma((4,)),
            dma, dma, dma, dma,
        ],
        compiler_params=pltpu.CompilerParams(
            collective_id=0, has_side_effects=True, vmem_limit_bytes=32 * 1024 * 1024
        ),
    )(
        displacement.reshape(3, rows, NX),
        velocity.reshape(3, rows, NX),
        body_force.reshape(3, rows, NX),
        modulus.reshape(rows, NX),
        damage_bits.reshape(2, rows, NX),
    )
    return u.reshape(displacement.shape), v.reshape(velocity.shape)


def solution(mesh):
    placed = (
        P(None, None, "gy", "gx"),
        P(None, None, "gy", "gx"),
        P(None, None, "gy", "gx"),
        P(None, "gy", "gx"),
        P(None, None, "gy", "gx"),
    )
    return jax.shard_map(
        shards,
        mesh=mesh,
        in_specs=placed,
        out_specs=(P(None, None, "gy", "gx"), P(None, None, "gy", "gx")),
        check_vma=False,
    )
```

time: 1300 us -> 64.8 us (0.05)
  local copies, waits for them, and re-layouts: 628 us -> 5.55 us
  blocking collectives: 496 us -> 0 us
  starting transfers between devices: 81.2 us -> 0 us
  Pallas kernels: 0 us -> 58.2 us
  waiting for transfers between devices: 47.5 us -> 0 us
  other arithmetic: 29.1 us -> 0 us
    scatter-add x90 -> x0, local copies, waits for them, and re-layouts: 622 us -> none  [the longest x80 565 us: bond_forces(): spread_forces = spread_forces.at[(slice(None),) + window].add(-bond_pull)]
    psum x4 -> x0, blocking collectives: 496 us -> none  [shards(): lax.psum((numerator_part, jnp.sum(velocity_now * velocity_now)), ('gx', '...]
    ppermute x30 -> x0, starting transfers between devices: 81.2 us -> none  [the longest x20 58.4 us: from_behind(): return lax.ppermute(block, axis, route)]
    pallas_call x0 -> x1, Pallas kernels: none -> 58.2 us  [shards(): pl.pallas_call(kernel, name='relax', out_shape=(out, out), in_specs=[pl.B...]
    ppermute x30 -> x0, waiting for transfers between devices: 47.5 us -> none  [the longest x20 37.7 us: from_behind(): return lax.ppermute(block, axis, route)]
  transfers between devices with their start and end apart: 30 -> 0, of which waited for: 15 -> 0; matrix products, arithmetic and copies ran while one was open for 10% -> 0% of each run, Pallas kernels for 0% -> 0%
where the time goes in v1:
time: 64.8 us; the launch traced here: 64.4 us
  Pallas kernels  58.2 us (90%)
  local copies, waits for them, and re-layouts  5.55 us (9%)
  between operations  0.65 us (1%)
    pallas_call x1, Pallas kernels, shards(): pl.pallas_call(kernel, name='relax', out_shape=(out, out), in_specs=[pl.B...  58.2 us
    unnamed x12, local copies, waits for them, and re-layouts  5.55 us

profile of v1, /device:TPU:1, one launch (start us, length us, event | category | flops | bytes accessed | tf_op | source)
XLA Modules:
  0.0 64.4 jit_solution(11789396414521728427)
XLA Ops:
  0.6 0.0 copy-start
  0.6 0.9 %copy-done = f32[3,8,8,128]{3,2,1,0:T(8,128)S(1)} copy-done((f32[3,8,8,128]{3,2,1,0:T(8,128)S(1)}, f32[3,8,8,128]{3,2,1,0:T(8,128)}, u32[]{:S(2)}) %copy-start) | copy-done | bytes 98328
  1.5 0.0 copy-start.1
  1.5 0.9 %copy-done.1 = f32[3,8,8,128]{3,2,1,0:T(8,128)S(1)} copy-done((f32[3,8,8,128]{3,2,1,0:T(8,128)S(1)}, f32[3,8,8,128]{3,2,1,0:T(8,128)}, u32[]{:S(2)}) %copy-start.1) | copy-done | bytes 98328
  2.4 0.0 copy-start.2
  2.4 0.9 %copy-done.2 = f32[3,8,8,128]{3,2,1,0:T(8,128)S(1)} copy-done((f32[3,8,8,128]{3,2,1,0:T(8,128)S(1)}, f32[3,8,8,128]{3,2,1,0:T(8,128)}, u32[]{:S(2)}) %copy-start.2) | copy-done | bytes 98328
  3.3 0.0 copy-start.3
  3.3 0.8 %copy-done.3 = s32[2,8,8,128]{3,2,1,0:T(8,128)S(1)} copy-done((s32[2,8,8,128]{3,2,1,0:T(8,128)S(1)}, s32[2,8,8,128]{3,2,1,0:T(8,128)}, u32[]{:S(2)}) %copy-start.3) | copy-done | bytes 65560
  4.2 0.0 copy-start.4
  4.2 0.8 %copy-done.4 = f32[8,8,128]{2,1,0:T(8,128)S(1)} copy-done((f32[8,8,128]{2,1,0:T(8,128)S(1)}, f32[8,8,128]{2,1,0:T(8,128)}, u32[]{:S(2)}) %copy-start.4) | copy-done | bytes 32792
  4.9 58.2 %relax.1 = (f32[3,64,128]{2,1,0:T(8,128)S(1)}, f32[3,64,128]{2,1,0:T(8,128)S(1)}) custom-call(f32[3,64,128]{2,1,0:T(8,128)S(1)} %bitcast.9, f32[3,64,128]{2,1,0:T(8,128)S(1)} %bitcast.10, f32[3,64,128]{2,1,0:T(8,128)S(1)} %bitcast.11, f32[64,128]{1,0:T(8,128)S(1)} %bitcast.13, s32[2,64,128]{2,1,0:T(8,128)S(1)} %bitcast.12), custom_call_target="tpu_custom_call" | custom-call | tf_op jit(solution)/shard_map/relax/pallas_call | solution.py:467
  63.1 0.6 copy.9
  63.8 0.6 copy.10
Async XLA Ops:
  0.6 0.9 %copy-start = (f32[3,8,8,128]{3,2,1,0:T(8,128)S(1)}, f32[3,8,8,128]{3,2,1,0:T(8,128)}, u32[]{:S(2)}) copy-start(f32[3,8,8,128]{3,2,1,0:T(8,128)} %param.5) | copy-start | bytes 294916
  1.5 0.9 %copy-start.1 = (f32[3,8,8,128]{3,2,1,0:T(8,128)S(1)}, f32[3,8,8,128]{3,2,1,0:T(8,128)}, u32[]{:S(2)}) copy-start(f32[3,8,8,128]{3,2,1,0:T(8,128)} %param.6) | copy-start | bytes 294916
  2.4 0.9 %copy-start.2 = (f32[3,8,8,128]{3,2,1,0:T(8,128)S(1)}, f32[3,8,8,128]{3,2,1,0:T(8,128)}, u32[]{:S(2)}) copy-start(f32[3,8,8,128]{3,2,1,0:T(8,128)} %param.7) | copy-start | bytes 294916
  3.3 0.8 %copy-start.3 = (s32[2,8,8,128]{3,2,1,0:T(8,128)S(1)}, s32[2,8,8,128]{3,2,1,0:T(8,128)}, u32[]{:S(2)}) copy-start(s32[2,8,8,128]{3,2,1,0:T(8,128)} %param.9) | copy-start | bytes 196612
  4.2 0.8 %copy-start.4 = (f32[8,8,128]{2,1,0:T(8,128)S(1)}, f32[8,8,128]{2,1,0:T(8,128)}, u32[]{:S(2)}) copy-start(f32[8,8,128]{2,1,0:T(8,128)} %param.8) | copy-start | bytes 98308

commit v2 on v1

--- a/solution.py
+++ b/solution.py
@@ -57,7 +57,7 @@
 def kernel(
     u_hbm, v_hbm, body_hbm, mod_hbm, bits_hbm, u_out, v_out,
     raw_u, raw_v, raw_body, raw_mod, raw_bits,
-    field, static, ahead, behind, ahead2, behind2, stiff, sides_static, last,
+    field, static, ahead, behind, ahead2, behind2, stiff, rims, sides_static, last,
     edge_out, edge_in, inner_in, static_in, moments, row_out, row_x, row_yz,
     load_sem, y_send, y_recv, e_send, e_recv, i_send, i_recv, s_send, s_recv, sy_send, sy_recv,
     rx_send, rx_recv, ryz_send, ryz_recv,
@@ -180,15 +180,17 @@
     edge = {-1: joined(static_in[0, 2], static_in[0, 3]), 0: joined(static_in[0, 0], static_in[0, 1]), 1: joined(static_in[0, 4], static_in[0, 5])}
     for y in range(-1, NY + 1):
         side = -1 if y < 0 else 1 if y >= NY else 0
-        row = y - side * NY
         for c in range(3):
-            value, halo = static[c, 2 + y], rim(edge[side], 3 * row + c)
+            rims[1, c, 1 + y] = rim(edge[side], 3 * (y - side * NY) + c)
+    for y in range(-1, NY + 1):
+        for c in range(3):
+            value, halo = static[c, 2 + y], rims[1, c, 1 + y]
             if c == 0:
                 ahead[1, 0, 0, 1 + y] = plus(value, halo, 1)
             behind[1, 0, c, 1 + y] = plus(value, halo, -1)
-            if side == 0 and c == 0:
+            if 0 <= y < NY and c == 0:
                 ahead2[1, 0, y] = plus(value, halo, 2)
-            if side == 0 and c != 1:
+            if 0 <= y < NY and c != 1:
                 behind2[1, c // 2, y] = plus(value, halo, -2)
 
     column_on = {}
@@ -248,10 +250,15 @@
 
     lax.fori_loop(0, NY, stiff_row, 0)
 
-    def widen(step, fields, y, edge_side, place):
+    def unpack(fields, y, edge_side, place):
         for f in fields:
             for c in range(3):
-                value, halo = field[step, f, c, 2 + y], rim(edge_side, place + 3 * f + c)
+                rims[f, c, 1 + y] = rim(edge_side, place + 3 * f + c)
+
+    def widen(step, fields, y):
+        for f in fields:
+            for c in range(3):
+                value, halo = field[step, f, c, 2 + y], rims[f, c, 1 + y]
                 ahead[0, f, c, 1 + y] = plus(value, halo, 1)
                 behind[0, f, c, 1 + y] = plus(value, halo, -1)
                 if c == 0 and 0 <= y < NY:
@@ -305,16 +312,14 @@
         return first[0] * second[0] + first[1] * second[1] + first[2] * second[2]
 
     def rows_pass(step, first_row):
-        body_on = jnp.where(step == 0, 1.0, 0.0).astype(F32)
-
         def row(index, sums):
             y = first_row(index)
             old_g, new_g = row_force(step, 0, y)
-            for c in range(3):
-                new_g[c] = new_g[c] + body_on * raw_body[c, pl.ds(y, NZ, stride=NY), :]
-                field[step + 1, 0, c, 2 + y] = new_g[c]
+            if step == 0:
+                new_g = [new_g[c] + raw_body[c, pl.ds(y, NZ, stride=NY), :] for c in range(3)]
             old_v, new_v = row_force(step, 1, y)
             for c in range(3):
+                field[step + 1, 0, c, 2 + y] = new_g[c]
                 field[step + 1, 1, c, 2 + y] = new_v[c]
             terms = [
                 dot(old_v, new_v), dot(new_v, new_v), dot(old_g, new_g),
@@ -331,13 +336,17 @@
         near_edge = joined(edge_in[step, 0], edge_in[step, 1])
         near_inner = joined(inner_in[step, 0], inner_in[step, 1])
         for place, y in enumerate(BOUNDARY):
-            widen(step, fields, y, near_edge, 6 * place)
+            unpack(fields, y, near_edge, 6 * place)
         for place, y in enumerate(INNER):
-            widen(step, fields, y, near_inner, 6 * place)
+            unpack(fields, y, near_inner, 6 * place)
+        for y in range(NY):
+            widen(step, fields, y)
         for copy in boundary_copies(step)[:4] + y_copies(step):
             copy.wait_recv()
-        widen(step, fields, -1, joined(edge_in[step, 2], edge_in[step, 3]), 18)
-        widen(step, fields, NY, joined(edge_in[step, 4], edge_in[step, 5]), 0)
+        unpack(fields, -1, joined(edge_in[step, 2], edge_in[step, 3]), 18)
+        unpack(fields, NY, joined(edge_in[step, 4], edge_in[step, 5]), 0)
+        widen(step, fields, -1)
+        widen(step, fields, NY)
 
     def outer_row(index):
         return index + 4 * (index // 2)
@@ -345,7 +354,7 @@
     def inner_row(index):
         return index + 2
 
-    def advance(step, carry):
+    def advance(step):
         arrive(step, (0, 1))
         outer = rows_pass(step, outer_row)
         for copy in y_copies(step + 1):
@@ -359,9 +368,9 @@
             copy.start()
         for place in range(6):
             moments[step * 6 + place] = outer[place] + inner[place]
-        return carry
-
-    lax.fori_loop(0, STEPS - 1, advance, 0)
+
+    for step in range(STEPS - 1):
+        advance(step)
 
     final = STEPS - 1
     arrive(final, (0,))
@@ -480,6 +489,7 @@
             vmem((2, 2, NY) + block, F32),
             vmem((2, 2, NY) + block, F32),
             vmem((len(FULL), NY) + block, F32),
+            vmem((2, 3, NY + 2) + block, F32),
             vmem(block, F32),
             vmem((3, NY) + block, F32),
             vmem((STEPS, 2) + block, F32),
@@ -499,7 +509,7 @@
             dma, dma, dma, dma,
         ],
         compiler_params=pltpu.CompilerParams(
-            collective_id=0, has_side_effects=True, vmem_limit_bytes=32 * 1024 * 1024
+            collective_id=0, has_side_effects=True, vmem_limit_bytes=60 * 1024 * 1024
         ),
     )(
         displacement.reshape(3, rows, NX),

time: 64.8 us -> 60.5 us (0.934)
  local copies, waits for them, and re-layouts: 5.55 us -> 2.22 us
  Pallas kernels: 58.2 us -> 57.4 us
    unnamed x12 -> x4, local copies, waits for them, and re-layouts: 5.55 us -> 2.22 us
    pallas_call x1, Pallas kernels: 58.2 us -> 57.4 us  [shards(): pl.pallas_call(kernel, name='relax', out_shape=(out, out), in_specs=[pl.B...]
where the time goes in v2:
time: 60.5 us; the launch traced here: 60.3 us
  Pallas kernels  57.4 us (95%)
  local copies, waits for them, and re-layouts  2.22 us (4%)
  between operations  0.65 us (1%)
    pallas_call x1, Pallas kernels, shards(): pl.pallas_call(kernel, name='relax', out_shape=(out, out), in_specs=[pl.B...  57.4 us
    unnamed x4, local copies, waits for them, and re-layouts  2.22 us

profile of v2, /device:TPU:1, one launch (start us, length us, event | category | flops | bytes accessed | tf_op | source)
XLA Modules:
  0.0 60.3 jit_solution(5544036348262875032)
XLA Ops:
  0.6 57.4 %relax.1 = (f32[3,64,128]{2,1,0:T(8,128)}, f32[3,64,128]{2,1,0:T(8,128)}) custom-call(f32[3,64,128]{2,1,0:T(8,128)} %bitcast.9, f32[3,64,128]{2,1,0:T(8,128)} %bitcast.10, f32[3,64,128]{2,1,0:T(8,128)} %bitcast.11, f32[64,128]{1,0:T(8,128)} %bitcast.13, s32[2,64,128]{2,1,0:T(8,128)} %bitcast.12), custom_call_target="tpu_custom_call" | custom-call | tf_op jit(solution)/shard_map/relax/pallas_call | solution.py:476
  58.0 0.0 copy-start
  58.0 1.6 %copy.9 = f32[3,8,8,128]{3,2,1,0:T(8,128)} copy(f32[3,8,8,128]{3,2,1,0:T(8,128)} %bitcast.8) | data formatting | bytes 196608
  59.6 0.0 copy-done
  59.6 0.6 %copy.10 = f32[3,8,8,128]{3,2,1,0:T(8,128)} copy(f32[3,8,8,128]{3,2,1,0:T(8,128)S(1)} %bitcast.7) | data formatting | bytes 196608
Async XLA Ops:
  58.0 1.6 %copy-start = (f32[3,64,128]{2,1,0:T(8,128)S(1)}, f32[3,64,128]{2,1,0:T(8,128)}, u32[]{:S(2)}) copy-start(f32[3,64,128]{2,1,0:T(8,128)} %get-tuple-element.5) | copy-start | bytes 294916

commit v3 on v1

v3 whole, which is shorter than its diff:
```python
import functools
import math

import jax
import jax.numpy as jnp
from jax import lax
from jax.experimental import pallas as pl
from jax.experimental.pallas import tpu as pltpu
from jax.sharding import PartitionSpec as P

ITERS = 4
NZ, NY, NX = 8, 8, 128
GX, GY, GZ = 16, 8, 8
MESH = pl.DeviceIdType.MESH
F32 = jnp.float32


def half_offsets():
    result = []
    for step_x in range(-2, 3):
        for step_y in range(-2, 3):
            for step_z in range(-2, 3):
                length_sq = step_x * step_x + step_y * step_y + step_z * step_z
                leading = step_x if step_x != 0 else step_y if step_y != 0 else step_z
                if 0 < length_sq <= 4 and leading > 0:
                    result.append((step_x, step_y, step_z))
    return result


HALF = half_offsets()
FULL = [(entry, number, 1) for number, entry in enumerate(HALF)] + [
    (tuple(-part for part in entry), number, -1) for number, entry in enumerate(HALF)
]
BOND = {entry: place for place, (entry, _, _) in enumerate(FULL)}
FICTIVE_MASS = 2.0 * sum(1.0 / math.sqrt(a * a + b * b + c * c) for a, b, c in HALF)

SIDES = [(-1, 0), (1, 0), (-1, -1), (1, -1), (-1, 1), (1, 1)]


def hops(distance, count):
    return min(distance % count, -distance % count)


CHIPS = GX // 2
X_STEPS = sorted(range(CHIPS), key=lambda d: -hops(d, CHIPS))
YZ_STEPS = sorted(
    [(dy, dz) for dy in range(GY) for dz in range(GZ) if dy or dz],
    key=lambda d: -(hops(d[0], GY) + hops(d[1], GZ)),
)

U, V0, G0, V1, G1, V2, G2, V3, G3 = range(9)
CHAIN_V, CHAIN_G = (V0, V1, V2, V3), (G0, G1, G2, G3)
EARLY = [(V0, V0), (V0, V1), (V1, V1), (G0, G0), (G0, G1), (G1, G1), (V0, G0), (V1, G0), (V1, G1)]
MIDDLE = [(V1, V2), (V2, V2), (V2, V3), (V2, G1)]
LATE = [(G1, G2), (G2, G2), (V2, G2), (V3, G2), (G2, G3)]
PAIRS = EARLY + MIDDLE + LATE
SLOTS = 24


def moment_slots(first, second):
    return [
        PAIRS.index(next((first[i], second[k - i]) for i in range(4) if 0 <= k - i < 4 and (first[i], second[k - i]) in PAIRS))
        for k in range(6)
    ]


VV, GG, VG = moment_slots(CHAIN_V, CHAIN_V), moment_slots(CHAIN_G, CHAIN_G), moment_slots(CHAIN_V, CHAIN_G)
REACH = 4
ROWS = NY + 2 * REACH
INNER = (2, 3, 4, 5)
OUTER = (-2, -1, 0, 1, 6, 7, 8, 9)


def kernel(
    u_hbm, v_hbm, body_hbm, mod_hbm, bits_hbm, result,
    raw_u, raw_v, raw_body, raw_mod, raw_bits,
    field, static, force, near_x, far_x, stiff, weights, edge_out, edge_in, moments, row_out, row_x, row_yz,
    load_sem, y_send, y_recv, side_send, side_recv, rx_send, rx_recv, ryz_send, ryz_recv, known,
):
    gx, gy = lax.axis_index("gx"), lax.axis_index("gy")
    part_y, part_z, core = gy // GZ, gy % GZ, gx % 2

    def near(dx, dy):
        return ((gx + dx + GX) % GX, (gy + dy + GY * GZ) % (GY * GZ))

    def across(dy, dz):
        return ((part_y + dy) % GY) * GZ + (part_z + dz) % GZ

    greeted = [near(dx, dy) for dx in (-1, 0, 1) for dy in (-1, 0, 1) if dx or dy]
    x_partners = [((gx + d) % GX, gy) for d in sorted(range(1, GX), key=lambda d: -hops(d, GX))]
    yz_partners = [(gx, across(dy, dz)) for dy, dz in YZ_STEPS]
    greeted += [near(dx, 0) for dx in (-2, 2)]
    boxes = [(dy, dz) for dy in (-1, 0, 1) for dz in (-1, 0, 1) if dy or dz]
    greeted += [(gx, across(dy, dz)) for dy, dz in boxes]
    rounds = [
        [near(dx * k, 0) for dx in (-2, 2)] + [(gx, across(dy * k, dz * k)) for dy, dz in boxes]
        for k in (1, 2)
    ]

    def call(number):
        for device in rounds[number]:
            pl.semaphore_signal(known.at[number], inc=1, device_id=device, device_id_type=MESH)

    def heard(number):
        pl.semaphore_wait(known.at[number], len(rounds[number]))

    barrier = pltpu.get_barrier_semaphore()

    def greet(devices):
        for device in devices:
            pl.semaphore_signal(barrier, inc=1, device_id=device, device_id_type=MESH)

    greet(greeted)
    loads = [
        pltpu.make_async_copy(source, target, load_sem.at[place])
        for place, (source, target) in enumerate(
            [(u_hbm, raw_u), (mod_hbm, raw_mod), (bits_hbm, raw_bits), (v_hbm, raw_v), (body_hbm, raw_body)]
        )
    ]
    for load in loads:
        load.start()

    lane = lax.broadcasted_iota(jnp.int32, (NZ, NX), 1)
    layer = lax.broadcasted_iota(jnp.int32, (NZ, NX), 0)
    nothing = jnp.zeros((NZ, NX), F32)

    def lanes_on(value, amount):
        return pltpu.roll(value, (-amount) % NX, axis=1)

    def layers_on(value, amount):
        return value if amount == 0 else pltpu.roll(value, (-amount) % NZ, axis=0)

    def plus(value, other, amount):
        if amount > 0:
            return lanes_on(jnp.where(lane < amount, other, value), amount)
        return lanes_on(jnp.where(lane >= NX + amount, other, value), amount)

    def pack(values, width, start=0):
        total = nothing
        for place, value in enumerate(values):
            turned = pltpu.roll(value, (8 * place + start + width) % NX, axis=1)
            total = jnp.where(lane // 8 == place, turned, total)
        return total

    def remote(source, target, send, recv, device):
        return pltpu.make_async_remote_copy(
            src_ref=source, dst_ref=target, send_sem=send, recv_sem=recv,
            device_id=device, device_id_type=MESH,
        )

    def row_copies(number):
        ref, deep, up, down = [
            (static.at[0], 4, slice(0, 2), slice(0, 1)),
            (field.at[U, 0], 4, slice(1, 2), slice(1, 2)),
            (field.at[V0, 0], 2, slice(1, 2), slice(1, 2)),
            (force.at[0], 2, slice(1, 2), slice(1, 2)),
            (field.at[V1, 0], 4, slice(1, 2), slice(1, 2)),
            (field.at[G1, 0], 4, slice(1, 2), slice(1, 2)),
        ][number]
        top, low = REACH + NY, REACH
        spans = [
            (slice(0, 3), slice(top - deep + 1, top), slice(low - deep + 1, low), 1),
            (slice(0, 3), slice(low, low + deep - 1), slice(top, top + deep - 1), -1),
            (up, slice(top - deep, top - deep + 1), slice(low - deep, low - deep + 1), 1),
            (down, slice(low + deep - 1, low + deep), slice(top + deep - 1, top + deep), -1),
        ]
        return [
            remote(ref.at[what, source], ref.at[what, target], y_send.at[number, place], y_recv.at[number, place], near(0, way))
            for place, (what, source, target, way) in enumerate(spans)
        ]

    def side_copies(group):
        first, last = [(0, 3), (3, 4), (4, 5)][group]
        copies = []
        for place, (dx, dy) in enumerate(SIDES):
            half = slice(0, 2) if dy == 0 else slice(1, 2) if dy < 0 else slice(0, 1)
            copies.append(
                remote(
                    edge_out.at[first:last, half], edge_in.at[first:last, place, half],
                    side_send.at[group, place], side_recv.at[group, place], near(-dx, -dy),
                )
            )
        return copies

    for load in loads:
        load.wait()
    for y in range(NY):
        turned = pl.ds(y, NZ, stride=NY)
        for c in range(3):
            field[U, 0, c, REACH + y] = raw_u[c, turned, :]
            field[V0, 0, c, REACH + y] = raw_v[c, turned, :]
            force[0, c, REACH + y] = raw_body[c, turned, :]
        static[0, 0, REACH + y] = raw_mod[turned, :]
        for c in range(2):
            static[0, 1 + c, REACH + y] = raw_bits[c, turned, :].astype(F32)

    def rows_of(ref, half):
        return [ref[c, REACH + 4 * half + y] for y in range(4) for c in range(3)]

    for half in range(2):
        edge_out[0, half] = pack(rows_of(static.at[0], half), 4)
        edge_out[1, half] = pack(rows_of(field.at[U, 0], half), 4)
        edge_out[2, half] = jnp.where(
            lane % 8 < 4, pack(rows_of(field.at[V0, 0], half), 2), pack(rows_of(force.at[0], half), 2, 4)
        )

    pl.semaphore_wait(barrier, len(greeted))
    for number in range(4):
        for copy in row_copies(number):
            copy.start()
        if number == 0:
            for copy in side_copies(0):
                copy.start()
    call(0)
    heard(0)
    call(1)

    def unpack(ref, number, half, sides, first, width, start=0, depth=4):
        both = jnp.where(
            lane % (2 * width) < width, edge_in[number, sides, half], edge_in[number, sides + 1, half]
        )
        for y in range(4):
            if first < 0 and y < 4 - depth or first >= NY and y >= depth:
                continue
            for c in range(3):
                slot = 8 * (3 * y + c) + start + width
                ref[c, REACH + first + y] = pltpu.roll(both, (2 * NX - slot) % NX, axis=1)

    def shift(value_ref, slot, rows, far_rows, kinds=(0, 1), comps=(0, 1, 2), ahead=(0, 1, 2), far=((0, 0, 0), (1, 0, 0))):
        for y in rows:
            row = REACH + y
            for e in kinds:
                for c in comps:
                    value, other = value_ref[e, c, row], value_ref[1 - e, c, row]
                    if c in ahead:
                        near_x[slot, e, 0, c, row] = plus(value, other, 1)
                    near_x[slot, e, 1, c, row] = plus(value, other, -1)
                    for way, which, place in far:
                        if which == c and y in far_rows:
                            far_x[slot, e, way, place, row] = plus(value, other, 2 - 4 * way)

    columns = {0: lane, 1: jnp.where(lane < NX // 2, lane + NX, lane - NX)}
    for e in range(2):
        for a in range(-2, 3):
            there = columns[e] + a
            on = jnp.logical_and(jnp.logical_or(gx > 0, there >= 0), jnp.logical_or(gx < GX - 1, there < NX))
            for c in range(-2, 3):
                if a * a + c * c <= 4:
                    inside = jnp.logical_and(layer + c >= 0, layer + c < NZ)
                    weights[e, 5 * (a + 2) + c + 2] = jnp.logical_and(on, inside).astype(F32)

    def stiff_row(y):
        row_on = {}
        for b in range(-2, 3):
            on = jnp.logical_and(
                jnp.logical_or(gy > 0, y + b >= 0), jnp.logical_or(gy < GY * GZ - 1, y + b < NY)
            )
            row_on[b] = jnp.where(on, 1.0, 0.0).astype(F32)
        for e in range(2):

            def at(c, a, b):
                row = REACH + y + b
                if a == 0:
                    return static[e, c, row]
                if abs(a) == 1:
                    return near_x[0, e, 0 if a > 0 else 1, c, row]
                return far_x[0, e, 0 if a > 0 else 1, 0 if c == 0 else 1, row]

            own = static[e, 0, REACH + y]
            words, partners, values = {}, {}, []
            for (a, b, c), number, sign in FULL:
                if (a, b, c) not in partners:
                    partners[a, b, c] = layers_on(at(0, a, b), c)
                length_sq = a * a + b * b + c * c
                scale = 0.5 / (length_sq * math.sqrt(length_sq)) * (4.0 if length_sq == 4 else 1.0)
                value = (own + partners[a, b, c]) * (weights[e, 5 * (a + 2) + c + 2] * (row_on[b] * scale))
                where = (number // 8, a, b) if sign < 0 else (number // 8, 0, 0)
                if where not in words:
                    words[where] = at(1 + where[0], where[1], where[2]).astype(jnp.int32)
                broken = jnp.bitwise_and(words[where], 1 << (number % 8))
                if sign < 0:
                    broken = layers_on(broken, c)
                values.append(jnp.where(broken == 0, value, 0.0))
            for place, value in enumerate(values):
                stiff[e, place, 2 + y] = value

    def pull(f, slot, e, y):
        row = REACH + y
        own = [field[f, e, c, row] for c in range(3)]
        total = [nothing, nothing, nothing]

        def bond(a, b, c):
            return stiff[e, BOND[a, b, c], 2 + y]

        for c in (-1, 1, -2, 2):
            total[2] += bond(0, 0, c) * (layers_on(own[2], c) - own[2])
        for b in (-1, 1):
            pair = [None if c == 0 else field[f, e, c, row + b] for c in range(3)]
            pulls = {}
            for gamma in (-1, 0, 1):
                c = gamma * b
                partner = pair[1] + gamma * pair[2] if gamma else pair[1]
                mine = own[1] + gamma * own[2] if gamma else own[1]
                pulls[gamma] = bond(0, b, c) * (layers_on(partner, c) - mine)
            total[1] += pulls[-1] + pulls[0] + pulls[1]
            total[2] += pulls[1] - pulls[-1]
        for b in (-2, 2):
            total[1] += bond(0, b, 0) * (field[f, e, 1, row + b] - own[1])
        for way in range(2):
            total[0] += bond(2 - 4 * way, 0, 0) * (far_x[slot, e, way, 0, row] - own[0])
        for beta in (-1, 0, 1):
            mine = own[0] + beta * own[1] if beta else own[0]
            for way, a in enumerate((1, -1)):
                b = a * beta
                pair = [near_x[slot, e, way, c, row + b] for c in range(3)]
                partner = pair[0] + beta * pair[1] if beta else pair[0]
                pulls = {}
                for gamma in (-1, 0, 1):
                    c = gamma * a
                    there = partner + gamma * pair[2] if gamma else partner
                    here = mine + gamma * own[2] if gamma else mine
                    pulls[gamma] = bond(a, b, c) * (layers_on(there, c) - here)
                both = pulls[-1] + pulls[0] + pulls[1]
                total[0] += both
                if beta:
                    total[1] += beta * both
                total[2] += pulls[1] - pulls[-1]
        return total

    def advance(f, slot, to, kinds, y):
        row = REACH + y
        news = [pull(f, slot, e, y) for e in kinds]
        if to == G0:
            news = [[new[c] + force[e, c, row] for c in range(3)] for e, new in zip(kinds, news)]
        for e, new in zip(kinds, news):
            for c in range(3):
                field[to, e, c, row] = new[c]

    def loop(count, where, *work):
        def one(index, carry):
            y = where(index)
            for step in work:
                step(y)
            return carry

        lax.fori_loop(0, count, one, 0)

    def inner(index):
        return index + 2

    def outer(index):
        return index - 2 + 4 * (index // 4)

    def rim(index):
        return index + 4 * (index // 2)

    def all_rows(index):
        return index

    def dot(first, second):
        return first[0] * second[0] + first[1] * second[1] + first[2] * second[2]

    def gather(pairs, last_step=None):
        used = sorted({f for pair in pairs for f in pair})

        def row(y, sums):
            if last_step is not None:
                last_step(y)
            have = {f: [field[f, 0, c, REACH + y] for c in range(3)] for f in used}
            return tuple(total + dot(have[a], have[b]) for total, (a, b) in zip(sums, pairs))

        sums = lax.fori_loop(0, NY, row, (nothing,) * len(pairs))
        for pair, total in zip(pairs, sums):
            moments[PAIRS.index(pair)] = total

    own_rows, outside = list(range(NY)), [-3, -2, -1, 8, 9, 10]
    wide_rows = set(range(-2, NY + 2))

    def halves(ref, number, width, start=0, depth=4, sides=(0,)):
        if 0 in sides:
            unpack(ref, number, 0, 0, 0, width, start)
            unpack(ref, number, 1, 0, 4, width, start)
        else:
            unpack(ref, number, 1, 2, -4, width, start, depth)
            unpack(ref, number, 0, 4, NY, width, start, depth)

    def shift_static(rows):
        shift(static, 0, rows, wide_rows, ahead=(0,), far=((0, 0, 0), (1, 0, 0), (1, 2, 1)))

    for copy in side_copies(0)[:2]:
        copy.wait_recv()
    halves(static.at[1], 0, 4)
    halves(field.at[U, 1], 1, 4)
    halves(field.at[V0, 1], 2, 2)
    halves(force.at[1], 2, 2, 4)
    shift_static(own_rows)
    shift(field.at[U], 1, own_rows, wide_rows)
    shift(field.at[V0], 2, own_rows, set(own_rows), kinds=(0,))
    loop(4, inner, stiff_row)
    loop(4, inner, lambda y: advance(V0, 2, V1, (0,), y), lambda y: advance(U, 1, G0, (0, 1), y))
    heard(1)
    for copy in side_copies(0)[2:] + row_copies(0) + row_copies(1) + row_copies(2) + row_copies(3):
        copy.wait_recv()
    halves(static.at[1], 0, 4, sides=(1,))
    halves(field.at[U, 1], 1, 4, sides=(1,))
    halves(field.at[V0, 1], 2, 2, depth=1, sides=(1,))
    halves(force.at[1], 2, 2, 4, depth=2, sides=(1,))
    shift_static(outside)
    shift(field.at[V0], 2, [-1, 8], set(), kinds=(0,))
    shift(field.at[U], 1, outside, wide_rows)
    loop(8, outer, stiff_row)
    loop(4, rim, lambda y: advance(V0, 2, V1, (0,), y))
    for copy in row_copies(4):
        copy.start()
    for half in range(2):
        edge_out[3, half] = pack(rows_of(field.at[V1, 0], half), 4)
    for copy in side_copies(1):
        copy.start()
    loop(8, outer, lambda y: advance(U, 1, G0, (0, 1), y))
    shift(field.at[G0], 3, [-1] + own_rows + [8], set(own_rows), kinds=(0,))
    loop(4, rim, lambda y: advance(G0, 3, G1, (0,), y))
    loop(4, inner, lambda y: advance(G0, 3, G1, (0,), y))
    for copy in row_copies(5):
        copy.start()
    for half in range(2):
        edge_out[4, half] = pack(rows_of(field.at[G1, 0], half), 4)
    for copy in side_copies(2):
        copy.start()

    gather(EARLY)
    for copy in side_copies(1) + row_copies(4):
        copy.wait_recv()
    for side in range(2):
        halves(field.at[V1, 1], 3, 4, sides=(side,))
    shift(field.at[V1], 4, own_rows + outside, wide_rows)
    loop(12, lambda index: index - 2, lambda y: advance(V1, 4, V2, (0, 1), y))
    shift(field.at[V2], 5, [-1] + own_rows + [8], set(own_rows), kinds=(0,))
    gather(MIDDLE, lambda y: advance(V2, 5, V3, (0,), y))
    for copy in side_copies(2)[:2]:
        copy.wait_recv()
    halves(field.at[G1, 1], 4, 4)
    shift(field.at[G1], 6, own_rows, wide_rows)
    loop(4, inner, lambda y: advance(G1, 6, G2, (0, 1), y))
    for copy in side_copies(2)[2:] + row_copies(5):
        copy.wait_recv()
    halves(field.at[G1, 1], 4, 4, sides=(1,))
    shift(field.at[G1], 6, outside, wide_rows)
    loop(8, outer, lambda y: advance(G1, 6, G2, (0, 1), y))
    shift(field.at[G2], 7, [-1] + own_rows + [8], set(own_rows), kinds=(0,))
    for place in range(len(PAIRS), SLOTS):
        moments[place] = nothing
    gather(LATE, lambda y: advance(G2, 7, G3, (0,), y))

    wide_lane = lax.broadcasted_iota(jnp.int32, (SLOTS, NX), 1)
    wide_row = lax.broadcasted_iota(jnp.int32, (SLOTS, NX), 0)
    summed = jnp.sum(jnp.sum(moments[...], axis=1), axis=1, keepdims=True)
    flat = jnp.sum(jnp.where(wide_lane == wide_row, summed, 0.0), axis=0, keepdims=True)

    def exchange(value, rows, partners, out, send, recv):
        count = len(partners)
        row_out[out, 0:1] = value
        rows[count : count + 1] = value
        for place, device in enumerate(partners):
            remote(row_out.at[out, 0:1], rows.at[place : place + 1], send, recv, device).start()
        whole = rows.at[0:count]
        pltpu.make_async_copy(whole, whole, recv).wait()
        return jnp.sum(rows[...], axis=0, keepdims=True)

    flat = exchange(flat, row_x, x_partners, 0, rx_send, rx_recv)
    flat = exchange(flat, row_yz, yz_partners, 1, ryz_send, ryz_recv)

    spread = jnp.sum(jnp.where(wide_lane == wide_row, jnp.broadcast_to(flat, (SLOTS, NX)), 0.0), axis=1, keepdims=True)
    spread = jnp.broadcast_to(spread, (SLOTS, NX))
    vv, gg, vg = ([spread[place : place + 1] for place in places] for places in (VV, GG, VG))

    zero = jnp.zeros((1, NX), F32)
    one = jnp.ones((1, NX), F32)
    speed_v, speed_g = [one, zero, zero, zero], [zero] * 4
    pull_v, pull_g = [zero] * 4, [one, zero, zero, zero]
    path_v, path_g = [zero] * 4, [zero] * 4
    for n in range(ITERS):
        terms = range(n if n else 1)

        def quadratic(order):
            total = zero
            for i in terms:
                for j in terms:
                    total = total + speed_v[i] * speed_v[j] * vv[i + j + order]
                    if n:
                        total = total + 2.0 * speed_v[i] * speed_g[j] * vg[i + j + order]
                        total = total + speed_g[i] * speed_g[j] * gg[i + j + order]
            return total

        denominator = quadratic(0)
        numerator = jnp.maximum(-quadratic(1) / FICTIVE_MASS, 0.0)
        damping = 2.0 * jnp.sqrt(numerator / (denominator + 1e-06))
        keep = (2.0 - damping) / (2.0 + damping)
        gain = 2.0 / (FICTIVE_MASS * (2.0 + damping))
        speed_v = [keep * x + gain * y for x, y in zip(speed_v, pull_v)]
        speed_g = [keep * x + gain * y for x, y in zip(speed_g, pull_g)]
        path_v = [x + y for x, y in zip(path_v, speed_v)]
        path_g = [x + y for x, y in zip(path_g, speed_g)]
        pull_v = [pull_v[0]] + [pull_v[j] + speed_v[j - 1] for j in range(1, 4)]
        pull_g = [pull_g[0]] + [pull_g[j] + speed_g[j - 1] for j in range(1, 4)]

    factors = [[jnp.broadcast_to(x, (NZ, NX)) for x in group] for group in (speed_v, speed_g, path_v, path_g)]

    def finish_row(y, carry):
        turned, row = pl.ds(y, NZ, stride=NY), REACH + y
        for c in range(3):
            basis = [field[f, 0, c, row] for f in CHAIN_V + CHAIN_G]
            result[1, c, turned, :] = sum(w * x for w, x in zip(factors[0] + factors[1], basis))
            moved = sum(w * x for w, x in zip(factors[2] + factors[3], basis))
            result[0, c, turned, :] = field[U, 0, c, row] + moved
        return carry

    lax.fori_loop(0, NY, finish_row, 0)
    for number in range(6):
        for copy in row_copies(number):
            copy.wait_send()
    for group in range(3):
        for copy in side_copies(group):
            copy.wait_send()

    for rows, count, sem in ((row_x, len(x_partners), rx_send), (row_yz, len(yz_partners), ryz_send)):
        whole = rows.at[0:count]
        pltpu.make_async_copy(whole, whole, sem).wait()


def part(both, u_out, v_out, sems):
    copies = [pltpu.make_async_copy(both.at[k], out, sems.at[k]) for k, out in enumerate((u_out, v_out))]
    for copy in copies:
        copy.start()
    for copy in copies:
        copy.wait()


def shards(displacement, velocity, body_force, modulus, damage_bits):
    rows = NZ * NY
    vmem = pltpu.VMEM
    dma = pltpu.SemaphoreType.DMA
    block = (NZ, NX)
    anywhere = pl.BlockSpec(memory_space=pl.ANY)
    out = jax.ShapeDtypeStruct((3, rows, NX), F32)
    both = pl.pallas_call(
        kernel,
        name="relax",
        out_shape=vmem((2, 3, rows, NX), F32),
        in_specs=[anywhere] * 5,
        out_specs=pl.BlockSpec(memory_space=vmem),
        scratch_shapes=[
            vmem((3, rows, NX), F32), vmem((3, rows, NX), F32), vmem((3, rows, NX), F32),
            vmem((rows, NX), F32), vmem((2, rows, NX), jnp.int32),
                        vmem((9, 2, 3, ROWS) + block, F32),
            vmem((2, 3, ROWS) + block, F32),
            vmem((2, 3, ROWS) + block, F32),
            vmem((8, 2, 2, 3, ROWS) + block, F32),
            vmem((8, 2, 2, 2, ROWS) + block, F32),
            vmem((2, len(FULL), NY + 4) + block, F32),
            vmem((2, 25) + block, F32),
            vmem((5, 2) + block, F32),
            vmem((5, 6, 2) + block, F32),
            vmem((SLOTS,) + block, F32),
            vmem((2, 8, NX), F32),
            vmem((GX, NX), F32),
            vmem((GY * GZ, NX), F32),
            dma((5,)),
            dma((6, 4)), dma((6, 4)),
            dma((3, 6)), dma((3, 6)),
            dma, dma, dma, dma,
            pltpu.SemaphoreType.REGULAR((2,)),
        ],
        compiler_params=pltpu.CompilerParams(
            collective_id=0, has_side_effects=True, vmem_limit_bytes=60 * 1024 * 1024
        ),
    )(
        displacement.reshape(3, rows, NX),
        velocity.reshape(3, rows, NX),
        body_force.reshape(3, rows, NX),
        modulus.reshape(rows, NX),
        damage_bits.reshape(2, rows, NX),
    )
    u, v = pl.pallas_call(
        part,
        name="part",
        out_shape=(out, out),
        in_specs=[pl.BlockSpec(memory_space=vmem)],
        out_specs=(anywhere, anywhere),
        scratch_shapes=[dma((2,))],
        compiler_params=pltpu.CompilerParams(vmem_limit_bytes=1024 * 1024),
    )(both)
    return u.reshape(displacement.shape), v.reshape(velocity.shape)


def solution(mesh):
    placed = (
        P(None, None, "gy", "gx"),
        P(None, None, "gy", "gx"),
        P(None, None, "gy", "gx"),
        P(None, "gy", "gx"),
        P(None, None, "gy", "gx"),
    )
    return jax.shard_map(
        shards,
        mesh=mesh,
        in_specs=placed,
        out_specs=(P(None, None, "gy", "gx"), P(None, None, "gy", "gx")),
        check_vma=False,
    )
```

time: 64.8 us -> 49.9 us (0.77)
  Pallas kernels: 58.2 us -> 49.1 us
  local copies, waits for them, and re-layouts: 5.55 us -> 0 us
    pallas_call x1 -> x2, Pallas kernels: 58.2 us -> 49.1 us  [the longest x1 48.4 us: shards(): pl.pallas_call(kernel, name='relax', out_shape=vmem((2, 3, rows, NX), F32...]
    unnamed x12 -> x0, local copies, waits for them, and re-layouts: 5.55 us -> none
where the time goes in v3:
time: 49.9 us; the launch traced here: 49.7 us
  Pallas kernels  49.1 us (98%)
  between operations  0.64 us (1%)
    pallas_call x1, Pallas kernels, shards(): pl.pallas_call(kernel, name='relax', out_shape=vmem((2, 3, rows, NX), F32...  48.4 us

profile of v3, /device:TPU:1, one launch (start us, length us, event | category | flops | bytes accessed | tf_op | source)
XLA Modules:
  0.0 49.7 jit_solution(3388216519353315872)
XLA Ops:
  0.6 48.4 %relax.1.both = f32[2,3,64,128]{3,2,1,0:T(8,128)S(1)} custom-call(f32[3,64,128]{2,1,0:T(8,128)} %bitcast.7, f32[3,64,128]{2,1,0:T(8,128)} %bitcast.8, f32[3,64,128]{2,1,0:T(8,128)} %bitcast.9, f32[64,128]{1,0:T(8,128)} %bitcast.11, s32[2,64,128]{2,1,0:T(8,128)} %bitcast.10), custom_call_target="tpu_custom_call" | custom-call | tf_op jit(solution)/shard_map/relax/pallas_call | solution.py:545
  49.0 0.7 %part.1 = (f32[3,64,128]{2,1,0:T(8,128)}, f32[3,64,128]{2,1,0:T(8,128)}) custom-call(f32[2,3,64,128]{3,2,1,0:T(8,128)S(1)} %relax.1.both), custom_call_target="tpu_custom_call" | custom-call | tf_op jit(solution)/shard_map/part/pallas_call | solution.py:583

commit v4 on v3

--- a/solution.py
+++ b/solution.py
@@ -67,8 +67,6 @@
 VV, GG, VG = moment_slots(CHAIN_V, CHAIN_V), moment_slots(CHAIN_G, CHAIN_G), moment_slots(CHAIN_V, CHAIN_G)
 REACH = 4
 ROWS = NY + 2 * REACH
-INNER = (2, 3, 4, 5)
-OUTER = (-2, -1, 0, 1, 6, 7, 8, 9)
 
 
 def kernel(
@@ -110,7 +108,6 @@
         for device in devices:
             pl.semaphore_signal(barrier, inc=1, device_id=device, device_id_type=MESH)
 
-    greet(greeted)
     loads = [
         pltpu.make_async_copy(source, target, load_sem.at[place])
         for place, (source, target) in enumerate(
@@ -119,6 +116,7 @@
     ]
     for load in loads:
         load.start()
+    greet(greeted)
 
     lane = lax.broadcasted_iota(jnp.int32, (NZ, NX), 1)
     layer = lax.broadcasted_iota(jnp.int32, (NZ, NX), 0)
@@ -212,8 +210,6 @@
             for copy in side_copies(0):
                 copy.start()
     call(0)
-    heard(0)
-    call(1)
 
     def unpack(ref, number, half, sides, first, width, start=0, depth=4):
         both = jnp.where(
@@ -249,14 +245,14 @@
                     inside = jnp.logical_and(layer + c >= 0, layer + c < NZ)
                     weights[e, 5 * (a + 2) + c + 2] = jnp.logical_and(on, inside).astype(F32)
 
-    def stiff_row(y):
+    def stiff_row(y, kinds=(0, 1)):
         row_on = {}
         for b in range(-2, 3):
             on = jnp.logical_and(
                 jnp.logical_or(gy > 0, y + b >= 0), jnp.logical_or(gy < GY * GZ - 1, y + b < NY)
             )
             row_on[b] = jnp.where(on, 1.0, 0.0).astype(F32)
-        for e in range(2):
+        for e in kinds:
 
             def at(c, a, b):
                 row = REACH + y + b
@@ -349,7 +345,10 @@
         return index + 2
 
     def outer(index):
-        return index - 2 + 4 * (index // 4)
+        return index - 1 + 4 * (index // 3)
+
+    def ends(index):
+        return 11 * index - 2
 
     def rim(index):
         return index + 4 * (index // 2)
@@ -398,17 +397,21 @@
     shift(field.at[V0], 2, own_rows, set(own_rows), kinds=(0,))
     loop(4, inner, stiff_row)
     loop(4, inner, lambda y: advance(V0, 2, V1, (0,), y), lambda y: advance(U, 1, G0, (0, 1), y))
-    heard(1)
-    for copy in side_copies(0)[2:] + row_copies(0) + row_copies(1) + row_copies(2) + row_copies(3):
+    heard(0)
+    call(1)
+    for copy in side_copies(0)[2:] + row_copies(0):
         copy.wait_recv()
     halves(static.at[1], 0, 4, sides=(1,))
     halves(field.at[U, 1], 1, 4, sides=(1,))
     halves(field.at[V0, 1], 2, 2, depth=1, sides=(1,))
     halves(force.at[1], 2, 2, 4, depth=2, sides=(1,))
     shift_static(outside)
+    loop(6, outer, stiff_row)
+    loop(2, ends, lambda y: stiff_row(y, (0,)))
+    for copy in row_copies(1) + row_copies(2):
+        copy.wait_recv()
     shift(field.at[V0], 2, [-1, 8], set(), kinds=(0,))
     shift(field.at[U], 1, outside, wide_rows)
-    loop(8, outer, stiff_row)
     loop(4, rim, lambda y: advance(V0, 2, V1, (0,), y))
     for copy in row_copies(4):
         copy.start()
@@ -416,7 +419,10 @@
         edge_out[3, half] = pack(rows_of(field.at[V1, 0], half), 4)
     for copy in side_copies(1):
         copy.start()
-    loop(8, outer, lambda y: advance(U, 1, G0, (0, 1), y))
+    for copy in row_copies(3):
+        copy.wait_recv()
+    loop(6, outer, lambda y: advance(U, 1, G0, (0, 1), y))
+    loop(2, ends, lambda y: advance(U, 1, G0, (0,), y))
     shift(field.at[G0], 3, [-1] + own_rows + [8], set(own_rows), kinds=(0,))
     loop(4, rim, lambda y: advance(G0, 3, G1, (0,), y))
     loop(4, inner, lambda y: advance(G0, 3, G1, (0,), y))
@@ -428,29 +434,36 @@
         copy.start()
 
     gather(EARLY)
-    for copy in side_copies(1) + row_copies(4):
-        copy.wait_recv()
-    for side in range(2):
-        halves(field.at[V1, 1], 3, 4, sides=(side,))
-    shift(field.at[V1], 4, own_rows + outside, wide_rows)
-    loop(12, lambda index: index - 2, lambda y: advance(V1, 4, V2, (0, 1), y))
-    shift(field.at[V2], 5, [-1] + own_rows + [8], set(own_rows), kinds=(0,))
-    gather(MIDDLE, lambda y: advance(V2, 5, V3, (0,), y))
+    for copy in side_copies(1)[:2]:
+        copy.wait_recv()
+    halves(field.at[V1, 1], 3, 4)
+    shift(field.at[V1], 4, own_rows, wide_rows)
+    loop(4, inner, lambda y: advance(V1, 4, V2, (0, 1), y))
     for copy in side_copies(2)[:2]:
         copy.wait_recv()
     halves(field.at[G1, 1], 4, 4)
     shift(field.at[G1], 6, own_rows, wide_rows)
     loop(4, inner, lambda y: advance(G1, 6, G2, (0, 1), y))
+    for copy in side_copies(1)[2:] + row_copies(4):
+        copy.wait_recv()
+    halves(field.at[V1, 1], 3, 4, sides=(1,))
+    shift(field.at[V1], 4, outside, wide_rows)
+    loop(6, outer, lambda y: advance(V1, 4, V2, (0, 1), y))
+    loop(2, ends, lambda y: advance(V1, 4, V2, (0,), y))
+    shift(field.at[V2], 5, [-1] + own_rows + [8], set(own_rows), kinds=(0,))
+    gather(MIDDLE, lambda y: advance(V2, 5, V3, (0,), y))
     for copy in side_copies(2)[2:] + row_copies(5):
         copy.wait_recv()
     halves(field.at[G1, 1], 4, 4, sides=(1,))
     shift(field.at[G1], 6, outside, wide_rows)
-    loop(8, outer, lambda y: advance(G1, 6, G2, (0, 1), y))
+    loop(6, outer, lambda y: advance(G1, 6, G2, (0, 1), y))
+    loop(2, ends, lambda y: advance(G1, 6, G2, (0,), y))
     shift(field.at[G2], 7, [-1] + own_rows + [8], set(own_rows), kinds=(0,))
     for place in range(len(PAIRS), SLOTS):
         moments[place] = nothing
     gather(LATE, lambda y: advance(G2, 7, G3, (0,), y))
 
+    heard(1)
     wide_lane = lax.broadcasted_iota(jnp.int32, (SLOTS, NX), 1)
     wide_row = lax.broadcasted_iota(jnp.int32, (SLOTS, NX), 0)
     summed = jnp.sum(jnp.sum(moments[...], axis=1), axis=1, keepdims=True)
@@ -482,14 +495,16 @@
         terms = range(n if n else 1)
 
         def quadratic(order):
-            total = zero
-            for i in terms:
-                for j in terms:
-                    total = total + speed_v[i] * speed_v[j] * vv[i + j + order]
-                    if n:
-                        total = total + 2.0 * speed_v[i] * speed_g[j] * vg[i + j + order]
-                        total = total + speed_g[i] * speed_g[j] * gg[i + j + order]
-            return total
+            parts = []
+            for total in range(2 * len(terms) - 1):
+                pairs = [(i, total - i) for i in terms if total - i in terms]
+                parts.append(sum(speed_v[i] * speed_v[j] for i, j in pairs) * vv[total + order])
+                if n:
+                    parts.append(sum(speed_v[i] * speed_g[j] for i, j in pairs) * (2.0 * vg[total + order]))
+                    parts.append(sum(speed_g[i] * speed_g[j] for i, j in pairs) * gg[total + order])
+            while len(parts) > 1:
+                parts = [parts[k] + parts[k + 1] if k + 1 < len(parts) else parts[k] for k in range(0, len(parts), 2)]
+            return parts[0]
 
         denominator = quadratic(0)
         numerator = jnp.maximum(-quadratic(1) / FICTIVE_MASS, 0.0)

time: 49.9 us -> 48.7 us (0.976)
  Pallas kernels: 49.1 us -> 47.8 us
    pallas_call x1, Pallas kernels: 48.4 us -> 47.1 us  [shards(): pl.pallas_call(kernel, name='relax', out_shape=vmem((2, 3, rows, NX), F32...]
where the time goes in v4:
time: 48.7 us; the launch traced here: 48.5 us
  Pallas kernels  47.8 us (98%)
  between operations  0.64 us (1%)
    pallas_call x1, Pallas kernels, shards(): pl.pallas_call(kernel, name='relax', out_shape=vmem((2, 3, rows, NX), F32...  47.1 us

profile of v4, /device:TPU:1, one launch (start us, length us, event | category | flops | bytes accessed | tf_op | source)
XLA Modules:
  0.0 48.5 jit_solution(10447784175137372860)
XLA Ops:
  0.6 47.1 %relax.1.both = f32[2,3,64,128]{3,2,1,0:T(8,128)S(1)} custom-call(f32[3,64,128]{2,1,0:T(8,128)} %bitcast.7, f32[3,64,128]{2,1,0:T(8,128)} %bitcast.8, f32[3,64,128]{2,1,0:T(8,128)} %bitcast.9, f32[64,128]{1,0:T(8,128)} %bitcast.11, s32[2,64,128]{2,1,0:T(8,128)} %bitcast.10), custom_call_target="tpu_custom_call" | custom-call | tf_op jit(solution)/shard_map/relax/pallas_call | solution.py:560
  47.8 0.7 %part.1 = (f32[3,64,128]{2,1,0:T(8,128)}, f32[3,64,128]{2,1,0:T(8,128)}) custom-call(f32[2,3,64,128]{3,2,1,0:T(8,128)S(1)} %relax.1.both), custom_call_target="tpu_custom_call" | custom-call | tf_op jit(solution)/shard_map/part/pallas_call | solution.py:598
